TPU v7x, 32 devices: a whole 2x2x4 slice. The times are simulated.
32 devices in a mesh: seq: 16 (over z, y, x), fsdp: 2 (over core).
Axes of the slice: x: 2, y: 2, z: 4, core: 2. Of those that a mesh axis runs over, the one named last changes fastest.
Arguments:
- queries: bfloat16 [4096, 2048], P(('seq', 'fsdp')), may hold values from -4.5 to 4.5
- keys: bfloat16 [4096, 2048], P(('seq', 'fsdp')), may hold values from -4.5 to 4.5
- values: bfloat16 [4096, 2048], P(('seq', 'fsdp')), may hold values from -6 to 6
- grad_out: bfloat16 [4096, 2048], P(('seq', 'fsdp')), may hold values from -6 to 6
- out_proj: bfloat16 [2048, 2048], P(('seq', 'fsdp')), may hold values from -0.125 to 0.125
- lists: int32 [16, 8], replicated, may hold values from 0 to 14, as said below
- window: int32 [16], replicated, may hold values from 64 to 128
Outputs:
- layer_out: bfloat16 [4096, 2048], P(('seq', 'fsdp'))
- grad_queries: bfloat16 [4096, 2048], P(('seq', 'fsdp'))
- grad_keys: bfloat16 [4096, 2048], P(('seq', 'fsdp'))
- grad_values: bfloat16 [4096, 2048], P(('seq', 'fsdp'))
Inputs may be any that keep to these rules, and one draw needn't show every extreme that they name: `lists`: within a row the ids are distinct; for b >= 1, row b holds the id b - 1.
All inputs are finite; a program needn't handle non-finite values.
Results may differ from a plain program's by a relative error of at most 0.025.
Values may be sent and summed in bfloat16 or wider, within the bound.
A program may use at most 128 MiB of HBM per device.

v0:
```python
import jax
import jax.numpy as jnp
from jax import lax
from jax.sharding import PartitionSpec as P

HEAD_DIM = 128
SUMMARY = 4
LISTED = 8


def passed_along(shard, axis, by):
    size = lax.axis_size(axis)
    pairs = [(i, i + by) for i in range(size) if 0 <= i + by < size]
    return lax.ppermute(shard, axis, pairs)


def from_root(block, axis, source):
    block = jnp.where(lax.axis_index(axis) == source, block, jnp.zeros_like(block))
    return lax.psum(block, axis)


def local(queries, keys, values, grad_out, out_proj, lists, window):
    f32 = jnp.float32
    tokens = queries.shape[0]
    att_width = queries.shape[1]
    heads = att_width // HEAD_DIM
    scale = 1.0 / HEAD_DIM**0.5
    blocks = lax.axis_size("seq")
    members = lax.axis_size("fsdp")
    block = lax.axis_index("seq")
    member = lax.axis_index("fsdp")
    first_dev = (block == 0) & (member == 0)
    nsum = blocks * SUMMARY
    nsel = LISTED * SUMMARY
    prev = passed_along(jnp.stack([keys, values]), ("seq", "fsdp"), 1)
    own_summary = jnp.stack([keys[tokens - SUMMARY :], values[tokens - SUMMARY :]])
    block_summary = from_root(own_summary, "fsdp", members - 1)
    summaries = lax.all_gather(block_summary, "seq", axis=1, tiled=True)
    block_ids = jnp.arange(blocks, dtype=jnp.int32)
    my_list = lax.dynamic_index_in_dim(lists, block, 0, keepdims=False)
    list_valid = my_list < block
    picked = jnp.take(summaries.reshape(2, blocks, SUMMARY, att_width), my_list, axis=1)
    sum_valid = jnp.repeat(list_valid, SUMMARY)
    q_heads = queries.reshape(tokens, heads, HEAD_DIM)
    key_loc = jnp.concatenate([prev[0], keys], axis=0).reshape(2 * tokens, heads, HEAD_DIM)
    val_loc = jnp.concatenate([prev[1], values], axis=0).reshape(2 * tokens, heads, HEAD_DIM)
    key_sum = picked[0].reshape(nsel, heads, HEAD_DIM)
    val_sum = picked[1].reshape(nsel, heads, HEAD_DIM)
    rows_t = jnp.arange(tokens, dtype=jnp.int32)
    rows_u = jnp.arange(2 * tokens, dtype=jnp.int32)
    offset = rows_t[:, None] + tokens - rows_u[None, :]
    extent = lax.dynamic_index_in_dim(window, block, 0, keepdims=False)
    loc_valid = (offset >= 0) & (offset < extent) & ((rows_u[None, :] >= tokens) | ~first_dev)
    score_loc = jnp.einsum("thd,uhd->htu", q_heads, key_loc, preferred_element_type=f32) * scale
    score_sum = jnp.einsum("thd,uhd->htu", q_heads, key_sum, preferred_element_type=f32) * scale
    top_loc = jnp.max(jnp.where(loc_valid[None], score_loc, -jnp.inf), axis=-1, keepdims=True)
    top_sum = jnp.max(
        jnp.where(sum_valid[None, None, :], score_sum, -jnp.inf), axis=-1, keepdims=True
    )
    top = jnp.maximum(top_loc, top_sum)
    expo_loc = jnp.where(loc_valid[None], jnp.exp(score_loc - top), 0.0)
    expo_sum = jnp.where(sum_valid[None, None, :], jnp.exp(score_sum - top), 0.0)
    total = jnp.sum(expo_loc, axis=-1, keepdims=True) + jnp.sum(expo_sum, axis=-1, keepdims=True)
    prob_loc = (expo_loc / total).astype(jnp.bfloat16)
    prob_sum = (expo_sum / total).astype(jnp.bfloat16)
    attn_f = jnp.einsum("htu,uhd->thd", prob_loc, val_loc, preferred_element_type=f32)
    attn_f = attn_f + jnp.einsum("htu,uhd->thd", prob_sum, val_sum, preferred_element_type=f32)
    attn = attn_f.reshape(tokens, att_width).astype(jnp.bfloat16)
    whole = lax.all_gather(out_proj, ("seq", "fsdp"), axis=0, tiled=True)
    layer_out = jnp.dot(attn, whole, preferred_element_type=f32).astype(jnp.bfloat16)
    grad_attn = lax.dot_general(
        grad_out, whole, (((1,), (1,)), ((), ())), preferred_element_type=f32
    ).astype(jnp.bfloat16)
    grad_heads = grad_attn.reshape(tokens, heads, HEAD_DIM)
    gprob_loc = jnp.einsum("thd,uhd->htu", grad_heads, val_loc, preferred_element_type=f32)
    gprob_sum = jnp.einsum("thd,uhd->htu", grad_heads, val_sum, preferred_element_type=f32)
    delta = jnp.sum(prob_loc * gprob_loc, axis=-1, keepdims=True) + jnp.sum(
        prob_sum * gprob_sum, axis=-1, keepdims=True
    )
    gscore_loc = (prob_loc * (gprob_loc - delta) * scale).astype(jnp.bfloat16)
    gscore_sum = (prob_sum * (gprob_sum - delta) * scale).astype(jnp.bfloat16)
    grad_q = jnp.einsum("htu,uhd->thd", gscore_loc, key_loc, preferred_element_type=f32)
    grad_q = grad_q + jnp.einsum("htu,uhd->thd", gscore_sum, key_sum, preferred_element_type=f32)
    grad_queries = grad_q.reshape(tokens, att_width).astype(jnp.bfloat16)
    gk_loc = jnp.einsum("htu,thd->uhd", gscore_loc, q_heads, preferred_element_type=f32).reshape(
        2 * tokens, att_width
    )
    gv_loc = jnp.einsum("htu,thd->uhd", prob_loc, grad_heads, preferred_element_type=f32).reshape(
        2 * tokens, att_width
    )
    gk_sum = jnp.einsum("htu,thd->uhd", gscore_sum, q_heads, preferred_element_type=f32).reshape(
        LISTED, SUMMARY * att_width
    )
    gv_sum = jnp.einsum("htu,thd->uhd", prob_sum, grad_heads, preferred_element_type=f32).reshape(
        LISTED, SUMMARY * att_width
    )
    placing = ((my_list[:, None] == block_ids[None, :]) & list_valid[:, None]).astype(f32)
    placed = jnp.einsum(
        "lb,xlc->xbc", placing, jnp.stack([gk_sum, gv_sum]), precision=lax.Precision.HIGHEST
    )
    placed = placed.reshape(2, nsum, att_width)
    returned = passed_along(
        jnp.stack([gk_loc[:tokens], gv_loc[:tokens]]).astype(jnp.bfloat16), ("seq", "fsdp"), -1
    ).astype(jnp.float32)
    column_part = lax.psum_scatter(
        placed.astype(jnp.bfloat16), "fsdp", scatter_dimension=2, tiled=True
    ).astype(jnp.float32)
    owned_part = lax.psum_scatter(column_part, "seq", scatter_dimension=1, tiled=True)
    block_part = lax.all_gather(owned_part, "fsdp", axis=2, tiled=True)
    owner = jnp.where(member == members - 1, 1.0, 0.0).astype(f32)
    extra = owner * jnp.pad(block_part, ((0, 0), (tokens - SUMMARY, 0), (0, 0)))
    grad_keys = (gk_loc[tokens:] + returned[0] + extra[0]).astype(jnp.bfloat16)
    grad_values = (gv_loc[tokens:] + returned[1] + extra[1]).astype(jnp.bfloat16)
    return (layer_out, grad_queries, grad_keys, grad_values)


def solution(mesh):
    in_specs = (
        P(("seq", "fsdp"), None),
        P(("seq", "fsdp"), None),
        P(("seq", "fsdp"), None),
        P(("seq", "fsdp"), None),
        P(("seq", "fsdp"), None),
        P(),
        P(),
    )
    out_specs = (
        P(("seq", "fsdp"), None),
        P(("seq", "fsdp"), None),
        P(("seq", "fsdp"), None),
        P(("seq", "fsdp"), None),
    )
    return jax.shard_map(local, mesh=mesh, in_specs=in_specs, out_specs=out_specs, check_vma=False)
```

profile of v0, /device:TPU:0, one launch (start us, length us, event | category | flops | bytes accessed | tf_op | source)
XLA Modules:
  0.0 237.6 jit_solution(4806070371253609222)
XLA Ops:
  7.2 0.7 all-gather.2.cloned.1.call-update
  8.0 1.3 copy.134
  9.3 1.3 copy.135
  10.6 1.2 pad_maximum_fusion
  11.8 3.3 %collective-permute-start = (bf16[2,128,2048]{1,2,0:T(8,128)(2,1)}, bf16[2,128,2048]{1,2,0:T(8,128)(2,1)}, u32[]{:S(2)}, u32[]{:S(2)}) collective-permute-start(bf16[2,128,2048]{1,2,0:T(8,128)(2,1)} %pad_maximum_fusion), channel_id=1, source_target_pairs={{0,1},{1,2},{2,3},{3,4},{4,5},{5,6},{6,7},{7,8},{8,9},{9,10},{10,1... | collective-permute-start | bytes 3145736 | tf_op jit(solution)/shard_map/ppermute | solution.py:14
  15.4 0.7 dynamic_slice.8
  16.4 0.8 slice_bitcast_fusion.4
  17.3 4.9 %psum.7 = bf16[2,4,2048]{2,1,0:T(4,128)(2,1)S(1)} all-reduce(bf16[2,4,2048]{2,1,0:T(4,128)(2,1)S(1)} %maximum_select_fusion), channel_id=1, replica_groups=mesh['seq'=16,'fsdp'=2] {'fsdp'}, use_global_device_ids=true, to_apply=%region_1.2 | all-reduce | flops 16384 | bytes 65536 | tf_op jit(solution)/shard_map/psum | solution.py:19
  22.2 44.9 %all_gather.9 = bf16[2,64,2048]{2,0,1:T(2,128)(2,1)S(1)} all-gather(bf16[2,4,2048]{2,0,1:T(2,128)(2,1)S(1)} %copy.141), channel_id=1, replica_groups=mesh['seq'=16,'fsdp'=2] {'seq'}, dimensions={1}, use_global_device_ids=true | all-gather | bytes 557056 | tf_op jit(solution)/shard_map/all_gather | solution.py:38
  67.4 0.8 gather_fusion
  68.7 0.6 dynamic-slice
  70.0 0.7 fusion.47
  70.7 1.1 select_reduce_fusion
  71.8 1.3 fusion.65
  73.5 0.5 fusion.4
  74.7 0.9 copy-done.5
  75.6 0.4 fusion.7
  76.1 21.1 %all-gather.2.cloned.1.call-done = bf16[2048,2048]{1,0:T(8,128)(2,1)} async-done(((bf16[64,2048]{1,0:T(8,128)(2,1)}), bf16[2048,2048]{1,0:T(8,128)(2,1)}) %all-gather.2.cloned.1.call-update) | async-done | bytes 8388624 | tf_op jit(solution)/shard_map/all_gather | solution.py:69
  97.1 6.4 %fusion.10 = bf16[16,16,8,128]{3,2,1,0:T(8,128)(2,1)S(1)} fusion(bf16[128,2048]{1,0:T(8,128)(2,1)S(1)} %copy-done.14, bf16[2048,2048]{1,0:T(8,128)(2,1)} %all-gather.2.cloned.1.call-done), kind=kOutput, calls=%fused_computation.24 | convolution fusion | flops 1074003968 | bytes 9437184 | tf_op jit(solution)/shard_map/dot_general | solution.py:71
  103.6 1.0 fusion.1
  104.6 0.5 convolution_bitcast_fusion
  105.1 1.0 slice.106
  106.0 0.4 fusion.40
  106.9 0.6 copy-done.9
  107.7 0.5 fusion.17
  108.2 0.5 convolution_bitcast_fusion.1
  108.7 1.0 slice.107
  110.2 1.0 convolution_bitcast_fusion.3
  111.2 1.1 fusion.9
  112.4 2.0 copy.168
  114.4 0.9 copy.166
  115.3 1.1 stack_reshape.7
  116.3 1.8 copy.164
  118.2 1.7 stack_reshape.6
  119.9 2.4 %fusion = bf16[2,16,8192]{2,1,0:T(8,128)(2,1)} fusion(f32[1,8,8192]{2,1,0:T(8,128)S(1)} %stack_reshape.7, f32[1,8,8192]{2,1,0:T(8,128)} %stack_reshape.6, s32[8]{0:T(128)S(1)} %dynamic-slice_reduce_fusion, pred[8]{0:T(512)(128)(4,1)S(1)} %get-tuple-element.34), kind=kOutput, calls=%fused_computation.2 | convolution fusion | flops 25559296 | bytes 1048616 | tf_op jit(solution)/shard_map/lb,xlc->xbc/dot_general | solution.py:98
  122.3 2.3 convert_element_type.86
  124.6 1.3 copy.167
  125.9 2.1 copy.161
  128.1 2.0 copy.160
  130.1 2.4 pad_maximum_fusion.3
  132.5 1.5 collective-permute-start.1
  133.9 1.4 copy.162
  135.7 1.5 fusion.8
  137.2 5.5 %convolution_convert_fusion.2 = bf16[128,2048]{1,0:T(8,128)(2,1)} fusion(bf16[128,2048]{0,1:T(8,128)(2,1)S(1)} %bitcast.152, bf16[2048,2048]{1,0:T(8,128)(2,1)} %all-gather.2.cloned.1.call-done), kind=kOutput, calls=%fused_computation.6 | convolution fusion | flops 1074003968 | bytes 9437184 | tf_op jit(solution)/shard_map/dot_general | solution.py:70
  142.7 82.7 %all-reduce.3 = f32[2,64,1024]{2,1,0:T(8,128)S(1)} all-reduce(bf16[2,64,1024]{2,1,0:T(8,128)(2,1)} %reduce-scatter.3.cloned.1.call-done), channel_id=3, replica_groups=mesh['seq'=16,'fsdp'=2] {'seq'}, use_global_device_ids=true, to_apply=%region_8.9.clone | all-reduce | flops 131072 | bytes 786432
  225.4 1.9 all_gather.11
  227.5 1.6 convert_element_type.83
  229.4 1.4 fusion.12
  (77 shorter events, 4.7 us)
Async XLA Ops:
  7.2 63.5 %copy-start = (bf16[128,2048]{1,0:T(8,128)(2,1)S(1)}, bf16[128,2048]{1,0:T(8,128)(2,1)}, u32[]{:S(2)}) copy-start(bf16[128,2048]{1,0:T(8,128)(2,1)} %param.7) | copy-start | bytes 1572868
  7.2 90.0 %all-gather.2.cloned.1.call-start = ((), (), s32[]{:S(2)}) async-start(), calls=%async_computation.1 | async-start | bytes 8650752 | tf_op jit(solution)/shard_map/all_gather | solution.py:69
  7.9 134.7 %reduce-scatter.3.cloned.1.call-start = ((), (), s32[]{:S(2)}) async-start(), calls=%async_computation.2 | async-start | bytes 786432 | tf_op jit(solution)/shard_map/reduce_scatter | solution.py:105
  9.3 6.1 %copy-start.19 = (s32[16]{0:T(128)S(1)}, s32[16]{0:T(128)}, u32[]{:S(2)}) copy-start(s32[16]{0:T(128)} %param.13) | copy-start | bytes 196
  9.3 6.8 %copy-start.18 = (s32[16,8]{0,1:T(8,128)S(1)}, s32[16,8]{0,1:T(8,128)}, u32[]{:S(2)}) copy-start(s32[16,8]{0,1:T(8,128)} %param.12) | copy-start | bytes 1540
  11.8 60.0 %collective-permute-start = (bf16[2,128,2048]{1,2,0:T(8,128)(2,1)}, bf16[2,128,2048]{1,2,0:T(8,128)(2,1)}, u32[]{:S(2)}, u32[]{:S(2)}) collective-permute-start(bf16[2,128,2048]{1,2,0:T(8,128)(2,1)} %pad_maximum_fusion), channel_id=1, source_target_pairs={{0,1},{1,2},{2,3},{3,4},{4,5},{5,6},{6,7},{7,8},{8,9},{9,10},{10,1... | collective-permute-start | bytes 3145736 | tf_op jit(solution)/shard_map/ppermute | solution.py:14
  15.4 58.0 %copy-start.8 = (bf16[128,16,128]{2,0,1:T(8,128)(2,1)}, bf16[128,16,128]{2,0,1:T(8,128)(2,1)S(1)}, u32[]{:S(2)}) copy-start(bf16[128,16,128]{2,0,1:T(8,128)(2,1)S(1)} %copy.139) | copy-start | bytes 1572868
  15.4 53.3 %copy-start.20 = (u32[32]{0:T(128)S(1)}, u32[32]{0:T(128)}, u32[]{:S(2)}) copy-start(u32[32]{0:T(128)} %constant.55) | copy-start | bytes 388
  68.6 4.6 %copy-start.12 = (bf16[32,16,128]{2,1,0:T(8,128)(2,1)}, bf16[32,16,128]{2,1,0:T(8,128)(2,1)S(1)}, u32[]{:S(2)}) copy-start(bf16[32,16,128]{2,1,0:T(8,128)(2,1)S(1)} %reshape_squeeze.6) | copy-start | bytes 393220
  68.7 37.4 %copy-start.15 = (bf16[32,16,128]{2,1,0:T(8,128)(2,1)}, bf16[32,16,128]{2,1,0:T(8,128)(2,1)S(1)}, u32[]{:S(2)}) copy-start(bf16[32,16,128]{2,1,0:T(8,128)(2,1)S(1)} %reshape_squeeze.7) | copy-start | bytes 393220
  73.1 30.4 %copy-start.7 = (bf16[1,128,2048]{1,2,0:T(8,128)(2,1)}, bf16[1,128,2048]{1,2,0:T(8,128)(2,1)S(1)}, u32[]{:S(2)}) copy-start(bf16[1,128,2048]{1,2,0:T(8,128)(2,1)S(1)} %get-tuple-element.30) | copy-start | bytes 1572868
  73.4 0.8 copy-start.10
  73.4 1.1 copy-start.17
  74.2 1.4 copy-start.5
  74.2 22.9 %copy-start.14 = (bf16[128,2048]{1,0:T(8,128)(2,1)S(1)}, bf16[128,2048]{1,0:T(8,128)(2,1)}, u32[]{:S(2)}) copy-start(bf16[128,2048]{1,0:T(8,128)(2,1)} %param.10) | copy-start | bytes 1572868
  97.1 6.4 %copy-start.6 = (f32[16,256,128]{2,1,0:T(8,128)S(1)}, f32[16,256,128]{2,1,0:T(8,128)}, u32[]{:S(2)}) copy-start(f32[16,256,128]{2,1,0:T(8,128)} %copy-done.5) | copy-start | bytes 6291460
  105.0 1.5 copy-start.2
  106.5 1.0 copy-start.9
  106.5 1.2 copy-start.11
  108.7 1.5 copy-start.1
  109.7 1.5 copy-start.13
  115.3 9.3 %slice-start.1 = ((f32[256,16,128]{0,2,1:T(8,128)}), f32[128,16,128]{0,2,1:T(8,128)S(1)}, s32[]{:S(2)}) async-start(f32[256,16,128]{0,2,1:T(8,128)} %copy-done.2), calls=%async_computation.4 | async-start | bytes 2097152 | tf_op jit(solution)/shard_map/slice | solution.py:113
  125.9 8.0 %slice-start = ((f32[256,16,128]{0,2,1:T(8,128)}), f32[128,16,128]{0,2,1:T(8,128)S(1)}, s32[]{:S(2)}) async-start(f32[256,16,128]{0,2,1:T(8,128)} %copy-done.1), calls=%async_computation.3 | async-start | bytes 2097152 | tf_op jit(solution)/shard_map/slice | solution.py:112
  130.1 5.2 %copy-start.16 = (bf16[32,16,128]{2,1,0:T(8,128)(2,1)S(1)}, bf16[32,16,128]{2,1,0:T(8,128)(2,1)}, u32[]{:S(2)}) copy-start(bf16[32,16,128]{2,1,0:T(8,128)(2,1)} %copy-done.15) | copy-start | bytes 393220
  132.5 95.1 %collective-permute-start.1 = (bf16[2,128,2048]{2,1,0:T(8,128)(2,1)}, bf16[2,128,2048]{2,1,0:T(8,128)(2,1)}, u32[]{:S(2)}, u32[]{:S(2)}) collective-permute-start(bf16[2,128,2048]{2,1,0:T(8,128)(2,1)} %pad_maximum_fusion.3), channel_id=1, source_target_pairs={{1,0},{2,1},{3,2},{4,3},{5,4},{6,5},{7,6},{8,7},{9,8},{10,9},{11,1... | collective-permute-start | bytes 3145736 | tf_op jit(solution)/shard_map/ppermute | solution.py:14
  227.5 1.6 copy-start.3
  227.5 1.8 copy-start.4
Sparse Core Ops, SparseCore 0:
  10.9 86.2 all-gather.1
  124.7 6.5 reduce-scatter.2
where the time goes:
time: 238 us
  blocking collectives  134 us (56%)
  local copies, waits for them, and re-layouts  29.9 us (13%)
  matrix products  22.9 us (10%)
  waiting for transfers between devices  21.8 us (9%)
  between operations  15.2 us (6%)
  other arithmetic  8.73 us (4%)
  starting transfers between devices  4.85 us (2%)
    unnamed x1, blocking collectives  82.7 us
    all_gather x1, blocking collectives, local(): summaries = lax.all_gather(block_summary, 'seq', axis=1, tiled=True)  44.9 us
    all_gather x1, waiting for transfers between devices, local(): whole = lax.all_gather(out_proj, ('seq', 'fsdp'), axis=0, tiled=True)  21.1 us
    unnamed x47, local copies, waits for them, and re-layouts  8.29 us
    dot_general x1, matrix products, local(): lax.dot_general(grad_out, whole, (((1,), (1,)), ((), ())), preferred_elem...  6.41 us
    dot_general x1, matrix products, local(): jnp.dot(attn, whole, preferred_element_type=f32).astype(jnp.bfloat16)  5.46 us
    psum x1, blocking collectives, from_root(): return lax.psum(block, axis)  4.9 us
    ppermute x2, starting transfers between devices, passed_along(): return lax.ppermute(shard, axis, pairs)  4.78 us
  transfers between devices with their start and end apart: 4, of which 1 were waited for; matrix products, arithmetic and copies ran while one was open for 12% of the time, Pallas kernels for 0%

commit v1 on v0

v1 whole, which is shorter than its diff:
```python
import functools

import jax
import jax.numpy as jnp
from jax import lax
from jax.experimental import pallas as pl
from jax.experimental.pallas import tpu as pltpu
from jax.sharding import PartitionSpec as P

HEAD_DIM = 128
SUMMARY = 4
MESH = pl.DeviceIdType.MESH
ANY = pl.BlockSpec(memory_space=pl.ANY)


def place():
    block, member = lax.axis_index("seq"), lax.axis_index("fsdp")
    return block, member, block * lax.axis_size("fsdp") + member


def fetch_kernel(
    blocks, members, k_ref, v_ref, own_ref, pk_ref, pv_ref, sum_ref,
    send_sem, recv_sem, prev_send, prev_recv, loc_sem,
):
    block, member, dev = place()
    ndev = blocks * members
    last = member == members - 1

    def to_next(i, src, dst):
        after = lax.rem(dev + 1, ndev)
        return pltpu.make_async_remote_copy(
            src_ref=src, dst_ref=dst, send_sem=prev_send.at[i], recv_sem=prev_recv.at[i],
            device_id=(after // members, lax.rem(after, members)), device_id_type=MESH,
        )

    def summary_to(i):
        to = lax.rem(dev + 1 + i, ndev)
        return pltpu.make_async_remote_copy(
            src_ref=own_ref, dst_ref=sum_ref.at[block], send_sem=send_sem.at[i],
            recv_sem=recv_sem.at[block],
            device_id=(to // members, lax.rem(to, members)), device_id_type=MESH,
        )

    local = pltpu.make_async_copy(own_ref, sum_ref.at[block], loc_sem)

    @pl.when(last)
    def _():
        local.start()

        @pl.loop(0, ndev - 1)
        def _(i):
            summary_to(i).start()

    next_k, next_v = to_next(0, k_ref, pk_ref), to_next(1, v_ref, pv_ref)
    next_k.start()
    next_v.start()

    @pl.when(last)
    def _():
        local.wait()

        @pl.loop(0, ndev - 1)
        def _(i):
            summary_to(i).wait_send()

    @pl.loop(0, blocks)
    def _(j):
        @pl.when(jnp.logical_not(last & (j == block)))
        def _():
            pltpu.make_async_remote_copy(
                src_ref=own_ref, dst_ref=sum_ref.at[j], send_sem=send_sem.at[0],
                recv_sem=recv_sem.at[j], device_id=(block, member), device_id_type=MESH,
            ).wait_recv()

    next_k.wait()
    next_v.wait()


def fetch(keys, values, own, blocks, members):
    ndev = blocks * members
    return pl.pallas_call(
        functools.partial(fetch_kernel, blocks, members),
        out_shape=(
            jax.ShapeDtypeStruct(keys.shape, keys.dtype),
            jax.ShapeDtypeStruct(values.shape, values.dtype),
            jax.ShapeDtypeStruct((blocks,) + own.shape, own.dtype),
        ),
        in_specs=[ANY] * 3,
        out_specs=(ANY,) * 3,
        scratch_shapes=[
            pltpu.SemaphoreType.DMA((ndev,)),
            pltpu.SemaphoreType.DMA((blocks,)),
            pltpu.SemaphoreType.DMA((2,)),
            pltpu.SemaphoreType.DMA((2,)),
            pltpu.SemaphoreType.DMA,
        ],
        compiler_params=pltpu.CompilerParams(has_side_effects=True),
        name="fetch",
    )(keys, values, own)


def give_back_kernel(
    blocks, members, ret_ref, gsum_ref, got_ref, parts_ref,
    send_sem, recv_sem, ret_send, ret_recv,
):
    block, member, dev = place()
    ndev = blocks * members
    before = lax.rem(dev + ndev - 1, ndev)
    back = pltpu.make_async_remote_copy(
        src_ref=ret_ref, dst_ref=got_ref, send_sem=ret_send, recv_sem=ret_recv,
        device_id=(before // members, lax.rem(before, members)), device_id_type=MESH,
    )

    def part_to(m):
        return pltpu.make_async_remote_copy(
            src_ref=gsum_ref.at[m], dst_ref=parts_ref.at[dev], send_sem=send_sem.at[m],
            recv_sem=recv_sem.at[dev], device_id=(m, members - 1), device_id_type=MESH,
        )

    @pl.loop(0, blocks)
    def _(m):
        @pl.when(m < block)
        def _():
            part_to(m).start()

    back.start()

    @pl.loop(0, blocks)
    def _(m):
        @pl.when(m < block)
        def _():
            part_to(m).wait_send()

    @pl.when(member == members - 1)
    def _():
        @pl.loop(0, ndev)
        def _(j):
            @pl.when(j >= (block + 1) * members)
            def _():
                pltpu.make_async_remote_copy(
                    src_ref=gsum_ref.at[0], dst_ref=parts_ref.at[j], send_sem=send_sem.at[0],
                    recv_sem=recv_sem.at[j], device_id=(block, member), device_id_type=MESH,
                ).wait_recv()

    back.wait()


def give_back(ret, gsum, blocks, members):
    ndev = blocks * members
    return pl.pallas_call(
        functools.partial(give_back_kernel, blocks, members),
        out_shape=(
            jax.ShapeDtypeStruct(ret.shape, ret.dtype),
            jax.ShapeDtypeStruct((ndev,) + gsum.shape[1:], gsum.dtype),
        ),
        in_specs=[ANY] * 2,
        out_specs=(ANY,) * 2,
        scratch_shapes=[
            pltpu.SemaphoreType.DMA((blocks,)),
            pltpu.SemaphoreType.DMA((ndev,)),
            pltpu.SemaphoreType.DMA,
            pltpu.SemaphoreType.DMA,
        ],
        compiler_params=pltpu.CompilerParams(has_side_effects=True),
        name="give_back",
    )(ret, gsum)


def dot(a, b, da, db):
    return lax.dot_general(a, b, (((da,), (db,)), ((), ())), preferred_element_type=jnp.float32)


def attend_kernel(
    q_ref, k_ref, v_ref, pk_ref, pv_ref, ks_ref, vs_ref, go_ref, w_ref, valid_ref,
    out_ref, gq_ref, gk_ref, gv_ref, ret_ref, gs_ref, total,
):
    f32, b16 = jnp.float32, jnp.bfloat16
    tokens = q_ref.shape[0]
    scale = 1.0 / HEAD_DIM**0.5
    h = pl.program_id(0)
    q, w = q_ref[...], w_ref[...]
    key = jnp.concatenate([pk_ref[...], k_ref[...], ks_ref[...]], axis=0)
    val = jnp.concatenate([pv_ref[...], v_ref[...], vs_ref[...]], axis=0)
    valid = valid_ref[...] > 0
    grad = dot(go_ref[...], w, 1, 1).astype(b16)
    score = jnp.where(valid, dot(q, key, 1, 1) * scale, -jnp.inf)
    top = jnp.max(score, axis=-1, keepdims=True)
    expo = jnp.exp(score - top)
    prob = (expo / jnp.sum(expo, axis=-1, keepdims=True)).astype(b16)
    attn = dot(prob, val, 1, 0).astype(b16)
    part = dot(attn, w, 1, 0)

    @pl.when(h == 0)
    def _():
        total[...] = part

    @pl.when(h > 0)
    def _():
        total[...] += part

    prob32 = prob.astype(f32)
    gprob = dot(grad, val, 1, 1)
    delta = jnp.sum(prob32 * gprob, axis=-1, keepdims=True)
    gscore = (prob32 * (gprob - delta) * scale).astype(b16)
    gq_ref[...] = dot(gscore, key, 1, 0).astype(b16)
    gk = dot(gscore, q, 0, 0)
    gv = dot(prob, grad, 0, 0)
    ret_ref[0] = gk[:tokens].astype(b16)
    ret_ref[1] = gv[:tokens].astype(b16)
    gk_ref[...] = gk[tokens : 2 * tokens]
    gv_ref[...] = gv[tokens : 2 * tokens]
    gs_ref[0] = gk[2 * tokens :].astype(b16)
    gs_ref[1] = gv[2 * tokens :].astype(b16)

    @pl.when(h == pl.num_programs(0) - 1)
    def _():
        out_ref[...] = total[...].astype(b16)


def attend(q, k, v, pk, pv, ks, vs, go, w, valid):
    tokens, width = q.shape
    nsum, wide = ks.shape[0], go.shape[1]
    f32, b16 = jnp.float32, jnp.bfloat16
    col = pl.BlockSpec((tokens, HEAD_DIM), lambda h: (0, h))
    scol = pl.BlockSpec((nsum, HEAD_DIM), lambda h: (0, h))
    whole = pl.BlockSpec((tokens, wide), lambda h: (0, 0))
    return pl.pallas_call(
        attend_kernel,
        grid=(width // HEAD_DIM,),
        in_specs=[
            col, col, col, col, col, scol, scol, whole,
            pl.BlockSpec((HEAD_DIM, wide), lambda h: (h, 0)),
            pl.BlockSpec(valid.shape, lambda h: (0, 0)),
        ],
        out_specs=(
            whole, col, col, col,
            pl.BlockSpec((2, tokens, HEAD_DIM), lambda h: (0, 0, h)),
            pl.BlockSpec((2, nsum, HEAD_DIM), lambda h: (0, 0, h)),
        ),
        out_shape=(
            jax.ShapeDtypeStruct((tokens, wide), b16),
            jax.ShapeDtypeStruct((tokens, width), b16),
            jax.ShapeDtypeStruct((tokens, width), f32),
            jax.ShapeDtypeStruct((tokens, width), f32),
            jax.ShapeDtypeStruct((2, tokens, width), b16),
            jax.ShapeDtypeStruct((2, nsum, width), b16),
        ),
        scratch_shapes=[pltpu.VMEM((tokens, wide), f32)],
        compiler_params=pltpu.CompilerParams(vmem_limit_bytes=32 * 2**20),
        name="attend",
    )(q, k, v, pk, pv, ks, vs, go, w, valid)


def local(queries, keys, values, grad_out, out_proj, lists, window):
    f32 = jnp.float32
    tokens, width = queries.shape
    blocks, members = lax.axis_size("seq"), lax.axis_size("fsdp")
    ndev = blocks * members
    block, member, dev = place()
    nsum = blocks * SUMMARY
    whole = lax.all_gather(out_proj, ("seq", "fsdp"), axis=0, tiled=True)
    own = jnp.stack([keys[tokens - SUMMARY :], values[tokens - SUMMARY :]])
    own = own.reshape(16, 2 * SUMMARY * width // 16)
    pk, pv, sums = fetch(keys, values, own, blocks, members)
    sums = sums.reshape(blocks, 2, SUMMARY, width)
    ks = sums[:, 0].reshape(nsum, width)
    vs = sums[:, 1].reshape(nsum, width)

    my_list = lax.dynamic_index_in_dim(lists, block, 0, keepdims=False)
    ids = jnp.arange(nsum, dtype=jnp.int32) // SUMMARY
    hit = jnp.any(my_list[:, None] == ids[None, :], axis=0) & (ids < block)
    extent = lax.dynamic_index_in_dim(window, block, 0, keepdims=False)
    rows = jnp.arange(tokens, dtype=jnp.int32)
    cols = jnp.arange(2 * tokens, dtype=jnp.int32)
    offset = rows[:, None] + tokens - cols[None, :]
    near = (offset >= 0) & (offset < extent) & ((cols[None, :] >= tokens) | (dev > 0))
    valid = jnp.concatenate([near, jnp.broadcast_to(hit[None], (tokens, nsum))], axis=1)

    out, gq, gk, gv, ret, gs = attend(
        queries, keys, values, pk, pv, ks, vs, grad_out, whole, valid.astype(f32)
    )
    gs = gs.reshape(2, blocks, SUMMARY, width).transpose(1, 0, 2, 3)
    got, parts = give_back(ret, gs.reshape(blocks, 16, -1), blocks, members)
    got = jnp.where(dev < ndev - 1, got.astype(f32), 0.0)
    sent = (jnp.arange(ndev) >= (block + 1) * members) & (member == members - 1)
    extra = jnp.sum(jnp.where(sent[:, None, None], parts.astype(f32), 0.0), axis=0)
    extra = extra.reshape(2, SUMMARY, width)
    pad = jnp.pad(extra, ((0, 0), (tokens - SUMMARY, 0), (0, 0)))
    grad_keys = (gk + got[0] + pad[0]).astype(jnp.bfloat16)
    grad_values = (gv + got[1] + pad[1]).astype(jnp.bfloat16)
    return out, gq, grad_keys, grad_values


def solution(mesh):
    split = P(("seq", "fsdp"), None)
    return jax.shard_map(
        local, mesh=mesh, in_specs=(split,) * 5 + (P(), P()), out_specs=(split,) * 4, check_vma=False
    )
```

time: 238 us -> 182 us (0.76)
  the two profiles are of different devices: /device:TPU:0 before, /device:TPU:15 now
where the time goes in v1:
time: 182 us; the launch traced here: 181 us
  Pallas kernels  94.3 us (52%)
  waiting for transfers between devices  50.8 us (28%)
  local copies, waits for them, and re-layouts  16.4 us (9%)
  between operations  14.2 us (8%)
  other arithmetic  5.23 us (3%)
    all_gather x1, waiting for transfers between devices, local(): whole = lax.all_gather(out_proj, ('seq', 'fsdp'), axis=0, tiled=True)  50.1 us
    pallas_call x1, Pallas kernels, fetch(): pl.pallas_call(functools.partial(fetch_kernel, blocks, members), out_shap...  38.4 us
    pallas_call x1, Pallas kernels, give_back(): pl.pallas_call(functools.partial(give_back_kernel, blocks, members), out_...  29.9 us
    pallas_call x1, Pallas kernels, attend(): pl.pallas_call(attend_kernel, grid=(width // HEAD_DIM,), in_specs=[col, c...  26 us
    unnamed x25, local copies, waits for them, and re-layouts  9.52 us
  transfers between devices with their start and end apart: 1, of which 1 were waited for; matrix products, arithmetic and copies ran while one was open for 3% of the time, Pallas kernels for 21%

profile of v1, /device:TPU:15, one launch (start us, length us, event | category | flops | bytes accessed | tf_op | source)
XLA Modules:
  0.0 181.0 jit_solution(17783427848842839436)
XLA Ops:
  7.2 0.0 copy-start
  7.2 0.0 all-gather.2.cloned.1.call-start
  7.2 0.7 all-gather.2.cloned.1.call-update
  7.9 1.2 dynamic_slice.8
  9.2 0.0 copy-done
  9.2 0.2 dynamic-slice_reduce_fusion
  9.4 0.8 slice_bitcast_fusion.4
  10.2 0.6 reshape.61.own_ref
  10.8 0.0 copy-start.2
  10.8 0.0 copy-start.3
  10.8 0.0 copy-start.7
  10.8 38.4 %fetch.1 = (bf16[128,2048]{1,0:T(8,128)(2,1)}, bf16[128,2048]{1,0:T(8,128)(2,1)}, bf16[16,16,1024]{2,1,0:T(8,128)(2,1)}) custom-call(bf16[128,2048]{1,0:T(8,128)(2,1)} %k_ref.3, bf16[128,2048]{1,0:T(8,128)(2,1)} %v_ref.3, bf16[16,1024]{1,0:T(8,128)(2,1)} %reshape.61.own_ref), custom_call_target="tpu_custom_call" | custom-call | tf_op jit(solution)/shard_map/fetch/pallas_call | solution.py:81
  49.2 1.4 reshape.62
  50.7 0.2 slice_bitcast_fusion.2
  50.9 0.1 reshape_squeeze.7.vs_ref
  51.0 0.1 reshape_squeeze.6.ks_ref
  51.0 0.1 compare_reduce_fusion
  51.2 0.7 fusion.11
  52.0 50.1 %all-gather.2.cloned.1.call-done.w_ref = bf16[2048,2048]{1,0:T(8,128)(2,1)} async-done(((bf16[64,2048]{1,0:T(8,128)(2,1)}), bf16[2048,2048]{1,0:T(8,128)(2,1)}) %all-gather.2.cloned.1.call-update) | async-done | bytes 8388624 | tf_op jit(solution)/shard_map/all_gather | solution.py:261
  102.1 0.0 copy-done.2
  102.1 0.0 copy-done.3
  102.1 0.0 copy-done.7
  102.1 0.0 copy-start.1
  102.1 3.4 %copy-done.1 = bf16[2048,2048]{1,0:T(8,128)(2,1)S(1)} copy-done((bf16[2048,2048]{1,0:T(8,128)(2,1)S(1)}, bf16[2048,2048]{1,0:T(8,128)(2,1)}, u32[]{:S(2)}) %copy-start.1) | copy-done | bytes 8388632
  105.5 0.0 copy-start.8
  105.5 1.0 copy-done.8
  106.5 0.0 copy-start.9
  106.5 1.0 copy-done.9
  107.6 0.0 copy-start.10
  107.6 1.0 copy-done.10
  108.6 26.0 %attend.1 = (bf16[128,2048]{1,0:T(8,128)(2,1)}, bf16[128,2048]{1,0:T(8,128)(2,1)}, f32[128,2048]{1,0:T(8,128)S(1)}, f32[128,2048]{1,0:T(8,128)S(1)}, bf16[2,128,...) custom-call(bf16[128,2048]{1,0:T(8,128)(2,1)S(1)} %copy-done.7, bf16[128,2048]{1,0:T(8,128)(2,1)S(1)} %copy-done.2, ...), custom_call_target="tpu_custom_call" | custom-call | tf_op jit(solution)/shard_map/attend/pallas_call | solution.py:227
  134.7 0.0 copy-start.4
  134.7 1.0 copy-done.4
  135.7 0.0 copy-start.5
  135.7 1.0 copy-done.5
  136.7 0.0 copy-start.11
  136.7 0.8 copy-done.11
  137.4 1.2 reshape.63
  138.7 0.2 copy.20
  138.9 0.9 reshape.64.gsum_ref
  139.9 29.9 %give_back.1 = (bf16[2,128,2048]{2,1,0:T(8,128)(2,1)}, bf16[32,16,1024]{2,1,0:T(8,128)(2,1)}) custom-call(bf16[2,128,2048]{2,1,0:T(8,128)(2,1)} %copy-done.4, bf16[16,16,1024]{2,1,0:T(8,128)(2,1)} %reshape.64.gsum_ref), custom_call_target="tpu_custom_call" | custom-call | tf_op jit(solution)/shard_map/give_back/pallas_call | solution.py:150
  169.7 0.0 copy-start.6
  169.8 1.6 select_reduce_fusion
  171.4 1.5 convert_select_fusion
  172.9 0.0 copy-done.6
  172.9 1.3 fusion.5
  (9 shorter events, 0.1 us)
Async XLA Ops:
  7.2 2.0 %copy-start = (s32[16,8]{0,1:T(8,128)S(1)}, s32[16,8]{0,1:T(8,128)}, u32[]{:S(2)}) copy-start(s32[16,8]{0,1:T(8,128)} %param.12) | copy-start | bytes 1540
  7.2 94.9 %all-gather.2.cloned.1.call-start = ((), (), s32[]{:S(2)}) async-start(), calls=%async_computation | async-start | bytes 8650752 | tf_op jit(solution)/shard_map/all_gather | solution.py:261
  10.8 91.3 %copy-start.2 = (bf16[128,2048]{1,0:T(8,128)(2,1)S(1)}, bf16[128,2048]{1,0:T(8,128)(2,1)}, u32[]{:S(2)}) copy-start(bf16[128,2048]{1,0:T(8,128)(2,1)} %k_ref.3) | copy-start | bytes 1572868
  10.8 91.3 %copy-start.3 = (bf16[128,2048]{1,0:T(8,128)(2,1)S(1)}, bf16[128,2048]{1,0:T(8,128)(2,1)}, u32[]{:S(2)}) copy-start(bf16[128,2048]{1,0:T(8,128)(2,1)} %v_ref.3) | copy-start | bytes 1572868
  10.8 91.3 %copy-start.7 = (bf16[128,2048]{1,0:T(8,128)(2,1)S(1)}, bf16[128,2048]{1,0:T(8,128)(2,1)}, u32[]{:S(2)}) copy-start(bf16[128,2048]{1,0:T(8,128)(2,1)} %q_ref.1) | copy-start | bytes 1572868
  102.1 3.4 %copy-start.1 = (bf16[2048,2048]{1,0:T(8,128)(2,1)S(1)}, bf16[2048,2048]{1,0:T(8,128)(2,1)}, u32[]{:S(2)}) copy-start(bf16[2048,2048]{1,0:T(8,128)(2,1)} %all-gather.2.cloned.1.call-done.w_ref) | copy-start | bytes 25165828
  105.5 1.0 copy-start.8
  106.5 1.0 copy-start.9
  107.6 1.0 copy-start.10
  134.7 1.0 copy-start.4
  135.7 1.0 copy-start.5
  136.7 0.8 copy-start.11
  169.7 3.1 %copy-start.6 = (f32[128,2048]{1,0:T(8,128)S(1)}, f32[128,2048]{1,0:T(8,128)}, u32[]{:S(2)}) copy-start(f32[128,2048]{1,0:T(8,128)} %copy-done.5) | copy-start | bytes 3145732
Sparse Core Ops, SparseCore 0:
  10.9 91.1 all-gather.1

commit v2 on v1

--- a/solution.py
+++ b/solution.py
@@ -8,6 +8,8 @@
 from jax.sharding import PartitionSpec as P
 
 HEAD_DIM = 128
+HEADS = 4
+CUTS = 2
 SUMMARY = 4
 MESH = pl.DeviceIdType.MESH
 ANY = pl.BlockSpec(memory_space=pl.ANY)
@@ -18,10 +20,129 @@
     return block, member, block * lax.axis_size("fsdp") + member
 
 
-def fetch_kernel(
-    blocks, members, k_ref, v_ref, own_ref, pk_ref, pv_ref, sum_ref,
-    send_sem, recv_sem, prev_send, prev_recv, loc_sem,
-):
+def ring_block(p, blocks):
+    if blocks != 16:
+        return p
+    col, up = p // 4, lax.rem(p, 4)
+    z = up + lax.rem(col, 2) * (3 - 2 * up)
+    return z * 4 + (col // 2) * 2 + lax.rem((col + 1) // 2, 2)
+
+
+def ring_place(block, blocks):
+    if blocks != 16:
+        return block
+    z, y, x = block // 4, lax.rem(block // 2, 2), lax.rem(block, 2)
+    col = 2 * y + lax.rem(x + y, 2)
+    return col * 4 + z + lax.rem(col, 2) * (3 - 2 * z)
+
+
+class Ring:
+    def __init__(self, blocks, w_ref, all_ref, sems):
+        self.block, self.member, self.dev = place()
+        self.blocks, self.w_ref, self.all_ref = blocks, w_ref, all_ref
+        self.f_send, self.f_recv, self.b_send, self.b_recv, self.s_send, self.s_recv, self.l_sem = sems
+        self.rows = w_ref.shape[0] // CUTS
+        self.me = ring_place(self.block, blocks)
+        self.f_count = blocks // 2 * CUTS
+        self.b_count = (blocks - 1 - blocks // 2) * CUTS
+
+    def chunk(self, block, member, c):
+        return self.all_ref.at[block * 2 + member, pl.ds(pl.multiple_of(c * self.rows, self.rows), self.rows)]
+
+    def copy(self, i, back, sends, recvs):
+        n, k = self.blocks, i // CUTS
+        shard = ring_block(lax.rem(self.me + n + (k if back else -k), n), n)
+        to = ring_block(lax.rem(self.me + n + (-1 if back else 1), n), n)
+        ref = self.chunk(shard, self.member, lax.rem(i, CUTS))
+        return pltpu.make_async_remote_copy(
+            src_ref=ref, dst_ref=ref, send_sem=sends.at[i], recv_sem=recvs.at[i],
+            device_id=(to, self.member), device_id_type=MESH,
+        )
+
+    def forward(self, i):
+        return self.copy(i, False, self.f_send, self.f_recv)
+
+    def backward(self, i):
+        return self.copy(i, True, self.b_send, self.b_recv)
+
+    def aside(self, block, c):
+        ref = self.chunk(block, self.member, c)
+        at = block * CUTS + c
+        return pltpu.make_async_remote_copy(
+            src_ref=ref, dst_ref=ref, send_sem=self.s_send.at[at], recv_sem=self.s_recv.at[at],
+            device_id=(self.block, 1 - self.member), device_id_type=MESH,
+        )
+
+    def arrived(self, j, back):
+        n, k = self.blocks, j // CUTS
+        shard = ring_block(lax.rem(self.me + n + (k + 1 if back else -k - 1), n), n)
+        c = lax.rem(j, CUTS)
+        ref = self.chunk(shard, self.member, c)
+        pltpu.make_async_remote_copy(
+            src_ref=ref, dst_ref=ref, send_sem=self.f_send.at[0],
+            recv_sem=(self.b_recv if back else self.f_recv).at[j],
+            device_id=(self.block, 1 - self.member), device_id_type=MESH,
+        ).wait_recv()
+        return shard, c
+
+    def run(self):
+        mine = pltpu.make_async_copy(self.w_ref, self.all_ref.at[self.dev], self.l_sem)
+        mine.start()
+        mine.wait()
+        for i in range(CUTS):
+            self.forward(i).start()
+            self.backward(i).start()
+        for c in range(CUTS):
+            self.aside(self.block, c).start()
+
+        @pl.loop(0, self.f_count)
+        def _(j):
+            shard, c = self.arrived(j, False)
+
+            @pl.when(j + CUTS < self.f_count)
+            def _():
+                self.forward(j + CUTS).start()
+
+            self.aside(shard, c).start()
+
+            @pl.when(j < self.b_count)
+            def _():
+                shard, c = self.arrived(j, True)
+
+                @pl.when(j + CUTS < self.b_count)
+                def _():
+                    self.backward(j + CUTS).start()
+
+                self.aside(shard, c).start()
+
+        @pl.loop(0, self.f_count)
+        def _(i):
+            self.forward(i).wait_send()
+
+        @pl.loop(0, self.b_count)
+        def _(i):
+            self.backward(i).wait_send()
+
+        @pl.loop(0, self.blocks * CUTS)
+        def _(a):
+            block, c = a // CUTS, lax.rem(a, CUTS)
+            self.aside(block, c).wait_send()
+            ref = self.chunk(block, 1 - self.member, c)
+            pltpu.make_async_remote_copy(
+                src_ref=ref, dst_ref=ref, send_sem=self.s_send.at[a], recv_sem=self.s_recv.at[a],
+                device_id=(self.block, 1 - self.member), device_id_type=MESH,
+            ).wait_recv()
+
+
+def fetch_kernel(blocks, members, ring, *refs):
+    if ring:
+        w_ref, refs = refs[0], refs[1:]
+        k_ref, v_ref, own_ref, all_ref = refs[:4]
+        refs = refs[4:]
+    else:
+        k_ref, v_ref, own_ref = refs[:3]
+        refs = refs[3:]
+    pk_ref, pv_ref, sum_ref, send_sem, recv_sem, prev_send, prev_recv, loc_sem = refs[:8]
     block, member, dev = place()
     ndev = blocks * members
     last = member == members - 1
@@ -54,6 +175,8 @@
     next_k, next_v = to_next(0, k_ref, pk_ref), to_next(1, v_ref, pv_ref)
     next_k.start()
     next_v.start()
+    if ring:
+        Ring(blocks, w_ref, all_ref, refs[8:]).run()
 
     @pl.when(last)
     def _():
@@ -76,27 +199,34 @@
     next_v.wait()
 
 
-def fetch(keys, values, own, blocks, members):
+def fetch(w, keys, values, own, blocks, members):
     ndev = blocks * members
-    return pl.pallas_call(
-        functools.partial(fetch_kernel, blocks, members),
-        out_shape=(
-            jax.ShapeDtypeStruct(keys.shape, keys.dtype),
-            jax.ShapeDtypeStruct(values.shape, values.dtype),
-            jax.ShapeDtypeStruct((blocks,) + own.shape, own.dtype),
-        ),
-        in_specs=[ANY] * 3,
-        out_specs=(ANY,) * 3,
-        scratch_shapes=[
-            pltpu.SemaphoreType.DMA((ndev,)),
-            pltpu.SemaphoreType.DMA((blocks,)),
-            pltpu.SemaphoreType.DMA((2,)),
-            pltpu.SemaphoreType.DMA((2,)),
-            pltpu.SemaphoreType.DMA,
-        ],
+    dma = pltpu.SemaphoreType.DMA
+    ring = members == 2 and blocks > 2 and w.shape[0] % (16 * CUTS) == 0
+    outs = (
+        jax.ShapeDtypeStruct(keys.shape, keys.dtype),
+        jax.ShapeDtypeStruct(values.shape, values.dtype),
+        jax.ShapeDtypeStruct((blocks,) + own.shape, own.dtype),
+    )
+    args = (keys, values, own)
+    sems = [dma((ndev,)), dma((blocks,)), dma((2,)), dma((2,)), dma]
+    if ring:
+        outs = (jax.ShapeDtypeStruct((ndev,) + w.shape, w.dtype),) + outs
+        args = (w,) + args
+        steps = blocks * CUTS
+        sems += [dma((steps,))] * 6 + [dma]
+    got = pl.pallas_call(
+        functools.partial(fetch_kernel, blocks, members, ring),
+        out_shape=outs,
+        in_specs=[ANY] * len(args),
+        out_specs=(ANY,) * len(outs),
+        scratch_shapes=sems,
         compiler_params=pltpu.CompilerParams(has_side_effects=True),
         name="fetch",
-    )(keys, values, own)
+    )(*args)
+    if ring:
+        return (got[0].reshape(ndev * w.shape[0], w.shape[1]),) + tuple(got[1:])
+    return (lax.all_gather(w, ("seq", "fsdp"), axis=0, tiled=True),) + tuple(got)
 
 
 def give_back_kernel(
@@ -117,13 +247,13 @@
             recv_sem=recv_sem.at[dev], device_id=(m, members - 1), device_id_type=MESH,
         )
 
+    back.start()
+
     @pl.loop(0, blocks)
     def _(m):
         @pl.when(m < block)
         def _():
             part_to(m).start()
-
-    back.start()
 
     @pl.loop(0, blocks)
     def _(m):
@@ -178,17 +308,34 @@
     tokens = q_ref.shape[0]
     scale = 1.0 / HEAD_DIM**0.5
     h = pl.program_id(0)
-    q, w = q_ref[...], w_ref[...]
-    key = jnp.concatenate([pk_ref[...], k_ref[...], ks_ref[...]], axis=0)
-    val = jnp.concatenate([pv_ref[...], v_ref[...], vs_ref[...]], axis=0)
+    w = w_ref[...]
     valid = valid_ref[...] > 0
-    grad = dot(go_ref[...], w, 1, 1).astype(b16)
-    score = jnp.where(valid, dot(q, key, 1, 1) * scale, -jnp.inf)
-    top = jnp.max(score, axis=-1, keepdims=True)
-    expo = jnp.exp(score - top)
-    prob = (expo / jnp.sum(expo, axis=-1, keepdims=True)).astype(b16)
-    attn = dot(prob, val, 1, 0).astype(b16)
-    part = dot(attn, w, 1, 0)
+    grads = dot(go_ref[...], w, 1, 1).astype(b16)
+    attns = []
+    for i in range(HEADS):
+        at = slice(i * HEAD_DIM, (i + 1) * HEAD_DIM)
+        q, grad = q_ref[:, at], grads[:, at]
+        key = jnp.concatenate([pk_ref[:, at], k_ref[:, at], ks_ref[:, at]], axis=0)
+        val = jnp.concatenate([pv_ref[:, at], v_ref[:, at], vs_ref[:, at]], axis=0)
+        score = jnp.where(valid, dot(q, key, 1, 1) * scale, -jnp.inf)
+        top = jnp.max(score, axis=-1, keepdims=True)
+        expo = jnp.exp(score - top)
+        prob = (expo / jnp.sum(expo, axis=-1, keepdims=True)).astype(b16)
+        attns.append(dot(prob, val, 1, 0).astype(b16))
+        prob32 = prob.astype(f32)
+        gprob = dot(grad, val, 1, 1)
+        delta = jnp.sum(prob32 * gprob, axis=-1, keepdims=True)
+        gscore = (prob32 * (gprob - delta) * scale).astype(b16)
+        gq_ref[:, at] = dot(gscore, key, 1, 0).astype(b16)
+        gk = dot(gscore, q, 0, 0)
+        gv = dot(prob, grad, 0, 0)
+        ret_ref[0, :, at] = gk[:tokens].astype(b16)
+        ret_ref[1, :, at] = gv[:tokens].astype(b16)
+        gk_ref[:, at] = gk[tokens : 2 * tokens]
+        gv_ref[:, at] = gv[tokens : 2 * tokens]
+        gs_ref[0, :, at] = gk[2 * tokens :].astype(b16)
+        gs_ref[1, :, at] = gv[2 * tokens :].astype(b16)
+    part = dot(jnp.concatenate(attns, axis=1), w, 1, 0)
 
     @pl.when(h == 0)
     def _():
@@ -197,20 +344,6 @@
     @pl.when(h > 0)
     def _():
         total[...] += part
-
-    prob32 = prob.astype(f32)
-    gprob = dot(grad, val, 1, 1)
-    delta = jnp.sum(prob32 * gprob, axis=-1, keepdims=True)
-    gscore = (prob32 * (gprob - delta) * scale).astype(b16)
-    gq_ref[...] = dot(gscore, key, 1, 0).astype(b16)
-    gk = dot(gscore, q, 0, 0)
-    gv = dot(prob, grad, 0, 0)
-    ret_ref[0] = gk[:tokens].astype(b16)
-    ret_ref[1] = gv[:tokens].astype(b16)
-    gk_ref[...] = gk[tokens : 2 * tokens]
-    gv_ref[...] = gv[tokens : 2 * tokens]
-    gs_ref[0] = gk[2 * tokens :].astype(b16)
-    gs_ref[1] = gv[2 * tokens :].astype(b16)
 
     @pl.when(h == pl.num_programs(0) - 1)
     def _():
@@ -221,21 +354,22 @@
     tokens, width = q.shape
     nsum, wide = ks.shape[0], go.shape[1]
     f32, b16 = jnp.float32, jnp.bfloat16
-    col = pl.BlockSpec((tokens, HEAD_DIM), lambda h: (0, h))
-    scol = pl.BlockSpec((nsum, HEAD_DIM), lambda h: (0, h))
+    step = HEADS * HEAD_DIM
+    col = pl.BlockSpec((tokens, step), lambda h: (0, h))
+    scol = pl.BlockSpec((nsum, step), lambda h: (0, h))
     whole = pl.BlockSpec((tokens, wide), lambda h: (0, 0))
     return pl.pallas_call(
         attend_kernel,
-        grid=(width // HEAD_DIM,),
+        grid=(width // step,),
         in_specs=[
             col, col, col, col, col, scol, scol, whole,
-            pl.BlockSpec((HEAD_DIM, wide), lambda h: (h, 0)),
+            pl.BlockSpec((step, wide), lambda h: (h, 0)),
             pl.BlockSpec(valid.shape, lambda h: (0, 0)),
         ],
         out_specs=(
             whole, col, col, col,
-            pl.BlockSpec((2, tokens, HEAD_DIM), lambda h: (0, 0, h)),
-            pl.BlockSpec((2, nsum, HEAD_DIM), lambda h: (0, 0, h)),
+            pl.BlockSpec((2, tokens, step), lambda h: (0, 0, h)),
+            pl.BlockSpec((2, nsum, step), lambda h: (0, 0, h)),
         ),
         out_shape=(
             jax.ShapeDtypeStruct((tokens, wide), b16),
@@ -246,7 +380,7 @@
             jax.ShapeDtypeStruct((2, nsum, width), b16),
         ),
         scratch_shapes=[pltpu.VMEM((tokens, wide), f32)],
-        compiler_params=pltpu.CompilerParams(vmem_limit_bytes=32 * 2**20),
+        compiler_params=pltpu.CompilerParams(vmem_limit_bytes=56 * 2**20),
         name="attend",
     )(q, k, v, pk, pv, ks, vs, go, w, valid)
 
@@ -258,10 +392,9 @@
     ndev = blocks * members
     block, member, dev = place()
     nsum = blocks * SUMMARY
-    whole = lax.all_gather(out_proj, ("seq", "fsdp"), axis=0, tiled=True)
     own = jnp.stack([keys[tokens - SUMMARY :], values[tokens - SUMMARY :]])
     own = own.reshape(16, 2 * SUMMARY * width // 16)
-    pk, pv, sums = fetch(keys, values, own, blocks, members)
+    whole, pk, pv, sums = fetch(out_proj, keys, values, own, blocks, members)
     sums = sums.reshape(blocks, 2, SUMMARY, width)
     ks = sums[:, 0].reshape(nsum, width)
     vs = sums[:, 1].reshape(nsum, width)

time: 182 us -> 145 us (0.80)
  waiting for transfers between devices: 50.8 us -> 0 us
  Pallas kernels: 94.3 us -> 130 us
  between operations: 14.2 us -> 0.79 us
  local copies, waits for them, and re-layouts: 16.4 us -> 8.5 us
    all_gather x1 -> x0, waiting for transfers between devices: 50.1 us -> none  [local(): whole = lax.all_gather(out_proj, ('seq', 'fsdp'), axis=0, tiled=True)]
    pallas_call x2, Pallas kernels: 64.4 us -> 97 us  [the longest x1 78 us: fetch(): pl.pallas_call(functools.partial(fetch_kernel, blocks, members, ring), ou...]
    unnamed x25 -> x7, local copies, waits for them, and re-layouts: 9.52 us -> 0.24 us
    pallas_call x1, Pallas kernels: 29.9 us -> 32.7 us  [give_back(): pl.pallas_call(functools.partial(give_back_kernel, blocks, members), out_...]
  transfers between devices with their start and end apart: 1 -> 0, of which waited for: 1 -> 0; matrix products, arithmetic and copies ran while one was open for 3% -> 0% of each run, Pallas kernels for 21% -> 0%
where the time goes in v2:
time: 145 us
  Pallas kernels  130 us (90%)
  local copies, waits for them, and re-layouts  8.5 us (6%)
  other arithmetic  6.01 us (4%)
    pallas_call x1, Pallas kernels, fetch(): pl.pallas_call(functools.partial(fetch_kernel, blocks, members, ring), ou...  78 us
    pallas_call x1, Pallas kernels, give_back(): pl.pallas_call(functools.partial(give_back_kernel, blocks, members), out_...  32.7 us
    pallas_call x1, Pallas kernels, attend(): pl.pallas_call(attend_kernel, grid=(width // step,), in_specs=[col, col,...  19 us

profile of v2, /device:TPU:15, one launch (start us, length us, event | category | flops | bytes accessed | tf_op | source)
XLA Modules:
  0.0 145.0 jit_solution(4111668182519386763)
XLA Ops:
  0.6 0.0 copy-start
  0.7 1.2 dynamic_slice.8
  1.9 0.0 copy-done
  1.9 0.2 dynamic-slice_reduce_fusion
  2.1 0.1 compare_reduce_fusion
  2.2 0.7 fusion.11
  3.0 0.8 slice_bitcast_fusion.4
  3.8 0.6 reshape.64.refs_3_
  4.5 0.7 add_convert_fusion.valid_ref
  5.2 78.0 %fetch.1 = (bf16[32,64,2048]{2,1,0:T(8,128)(2,1)}, bf16[128,2048]{1,0:T(8,128)(2,1)}, bf16[128,2048]{1,0:T(8,128)(2,1)}, bf16[16,16,1024]{2,1,0:T(8,128)(2,1)}) custom-call(bf16[64,2048]{1,0:T(8,128)(2,1)} %refs_0_.1, bf16[128,2048]{1,0:T(8,128)(2,1)} %k_ref.1, bf16[128,2048]{1,0:T(8,128)(2,1)} %v_ref.1, bf16[16,1024]{1,0:T(8,128)(2,1)} %reshape.64.refs_3_), custom_call_target="tpu_custom_call" | custom-call | tf_op jit(solution)/shard_map/fetch/pallas_call | solution.py:218
  83.2 1.4 reshape.65
  84.6 0.2 slice_bitcast_fusion.2
  84.8 0.8 reshape_squeeze.7.vs_ref
  85.6 0.8 reshape_squeeze.6.ks_ref
  86.4 19.0 %attend.1 = (bf16[128,2048]{1,0:T(8,128)(2,1)}, bf16[128,2048]{1,0:T(8,128)(2,1)}, f32[128,2048]{1,0:T(8,128)}, f32[128,2048]{1,0:T(8,128)}, bf16[2,128,2048]{2,...) custom-call(bf16[128,2048]{1,0:T(8,128)(2,1)} %q_ref.1, bf16[128,2048]{1,0:T(8,128)(2,1)} %k_ref.1, bf16[128,2048]{1,0:T(8,128)(2,1)} %v_ref.1, ...), custom_call_target="tpu_custom_call" | custom-call | tf_op jit(solution)/shard_map/attend/pallas_call | solution.py:361
  105.4 1.2 reshape.67
  106.6 0.2 copy.20
  106.9 0.9 reshape.68.gsum_ref
  107.8 32.7 %give_back.1 = (bf16[2,128,2048]{2,1,0:T(8,128)(2,1)}, bf16[32,16,1024]{2,1,0:T(8,128)(2,1)}) custom-call(bf16[2,128,2048]{2,1,0:T(8,128)(2,1)} %get-tuple-element.23.ret_ref, bf16[16,16,1024]{2,1,0:T(8,128)(2,1)} %reshape.68.gsum_ref), custom_call_target="tpu_custom_call" | custom-call | tf_op jit(solution)/shard_map/give_back/pallas_call | solution.py:280
  140.5 0.0 copy-start.1
  140.5 0.0 copy-start.2
  140.5 1.6 %select_reduce_fusion = f32[16,1024]{1,0:T(8,128)S(1)} fusion(bf16[32,16,1024]{2,1,0:T(8,128)(2,1)} %get-tuple-element.26, pred[32]{0:T(512)(128)(4,1)S(1)} %compare_and_fusion), kind=kLoop, calls=%fused_computation.2 | loop fusion | flops 1556480 | bytes 1114144 | tf_op jit(solution)/shard_map/reduce_sum | solution.py:419
  142.2 1.5 %convert_select_fusion = f32[2,128,2048]{2,1,0:T(8,128)S(1)} fusion(bf16[2,128,2048]{2,1,0:T(8,128)(2,1)} %get-tuple-element.25, pred[]{:T(512)S(6)} %lt.30), kind=kLoop, calls=%fused_computation.3 | loop fusion | flops 1048576 | bytes 3145729 | tf_op jit(solution)/shard_map/jit(_where)/select_n | solution.py:417
  143.7 0.0 copy-done.1
  143.7 0.0 copy-done.2
  143.7 1.3 fusion.5
  (8 shorter events, 0.1 us)
Async XLA Ops:
  0.6 1.3 copy-start
  140.5 3.2 %copy-start.1 = (f32[128,2048]{1,0:T(8,128)S(1)}, f32[128,2048]{1,0:T(8,128)}, u32[]{:S(2)}) copy-start(f32[128,2048]{1,0:T(8,128)} %get-tuple-element.22) | copy-start | bytes 3145732
  140.5 3.2 %copy-start.2 = (f32[128,2048]{1,0:T(8,128)S(1)}, f32[128,2048]{1,0:T(8,128)}, u32[]{:S(2)}) copy-start(f32[128,2048]{1,0:T(8,128)} %get-tuple-element.27) | copy-start | bytes 3145732

commit v3 on v2

--- a/solution.py
+++ b/solution.py
@@ -9,7 +9,6 @@
 
 HEAD_DIM = 128
 HEADS = 4
-CUTS = 2
 SUMMARY = 4
 MESH = pl.DeviceIdType.MESH
 ANY = pl.BlockSpec(memory_space=pl.ANY)
@@ -20,122 +19,129 @@
     return block, member, block * lax.axis_size("fsdp") + member
 
 
-def ring_block(p, blocks):
-    if blocks != 16:
-        return p
-    col, up = p // 4, lax.rem(p, 4)
-    z = up + lax.rem(col, 2) * (3 - 2 * up)
-    return z * 4 + (col // 2) * 2 + lax.rem((col + 1) // 2, 2)
-
-
-def ring_place(block, blocks):
-    if blocks != 16:
-        return block
-    z, y, x = block // 4, lax.rem(block // 2, 2), lax.rem(block, 2)
-    col = 2 * y + lax.rem(x + y, 2)
-    return col * 4 + z + lax.rem(col, 2) * (3 - 2 * z)
-
-
-class Ring:
-    def __init__(self, blocks, w_ref, all_ref, sems):
+class Grid:
+    def __init__(self, w_ref, all_ref, sems):
         self.block, self.member, self.dev = place()
-        self.blocks, self.w_ref, self.all_ref = blocks, w_ref, all_ref
-        self.f_send, self.f_recv, self.b_send, self.b_recv, self.s_send, self.s_recv, self.l_sem = sems
-        self.rows = w_ref.shape[0] // CUTS
-        self.me = ring_place(self.block, blocks)
-        self.f_count = blocks // 2 * CUTS
-        self.b_count = (blocks - 1 - blocks // 2) * CUTS
-
-    def chunk(self, block, member, c):
-        return self.all_ref.at[block * 2 + member, pl.ds(pl.multiple_of(c * self.rows, self.rows), self.rows)]
-
-    def copy(self, i, back, sends, recvs):
-        n, k = self.blocks, i // CUTS
-        shard = ring_block(lax.rem(self.me + n + (k if back else -k), n), n)
-        to = ring_block(lax.rem(self.me + n + (-1 if back else 1), n), n)
-        ref = self.chunk(shard, self.member, lax.rem(i, CUTS))
+        self.z, self.y, self.x = self.block // 4, lax.rem(self.block // 2, 2), lax.rem(self.block, 2)
+        self.w_ref, self.all_ref, self.rows = w_ref, all_ref, w_ref.shape[0] // 2
+        (self.z_send, self.z_recv, self.x_send, self.x_recv, self.y_send, self.y_recv, self.dx_send,
+         self.dx_recv, self.dy_send, self.dy_recv, self.s_send, self.s_recv, self.l_sem) = sems
+
+    def at(self, z, dy=0, dx=0):
+        y = 1 - self.y if dy else self.y
+        x = 1 - self.x if dx else self.x
+        return z * 4 + y * 2 + x
+
+    def ref(self, block, half=None, other=False):
+        shard = block * 2 + (1 - self.member if other else self.member)
+        if half is None:
+            return self.all_ref.at[shard]
+        return self.all_ref.at[shard, pl.ds(half * self.rows, self.rows)]
+
+    def copy(self, ref, to, send, recv):
         return pltpu.make_async_remote_copy(
-            src_ref=ref, dst_ref=ref, send_sem=sends.at[i], recv_sem=recvs.at[i],
+            src_ref=ref, dst_ref=ref, send_sem=send, recv_sem=recv,
             device_id=(to, self.member), device_id_type=MESH,
         )
 
-    def forward(self, i):
-        return self.copy(i, False, self.f_send, self.f_recv)
-
-    def backward(self, i):
-        return self.copy(i, True, self.b_send, self.b_recv)
-
-    def aside(self, block, c):
-        ref = self.chunk(block, self.member, c)
-        at = block * CUTS + c
+    def arrived(self, ref, recv):
+        self.copy(ref, self.at(self.z, dx=1), self.x_send.at[0], recv).wait_recv()
+
+    def aside(self, block, half=None, other=False):
+        ref = self.ref(block, half, other)
+        i = block * 2 + (half or 0)
         return pltpu.make_async_remote_copy(
-            src_ref=ref, dst_ref=ref, send_sem=self.s_send.at[at], recv_sem=self.s_recv.at[at],
+            src_ref=ref, dst_ref=ref, send_sem=self.s_send.at[i], recv_sem=self.s_recv.at[i],
             device_id=(self.block, 1 - self.member), device_id_type=MESH,
         )
 
-    def arrived(self, j, back):
-        n, k = self.blocks, j // CUTS
-        shard = ring_block(lax.rem(self.me + n + (k + 1 if back else -k - 1), n), n)
-        c = lax.rem(j, CUTS)
-        ref = self.chunk(shard, self.member, c)
-        pltpu.make_async_remote_copy(
-            src_ref=ref, dst_ref=ref, send_sem=self.f_send.at[0],
-            recv_sem=(self.b_recv if back else self.f_recv).at[j],
-            device_id=(self.block, 1 - self.member), device_id_type=MESH,
-        ).wait_recv()
-        return shard, c
+    def up(self, z):
+        return self.copy(self.ref(self.at(z)), self.at(self.z + 1), self.z_send.at[z], self.z_recv.at[z])
+
+    def down(self, z):
+        return self.copy(self.ref(self.at(z)), self.at(self.z - 1), self.z_send.at[4 + z], self.z_recv.at[z])
+
+    def to_x(self, z):
+        return self.copy(self.ref(self.at(z)), self.at(self.z, dx=1), self.x_send.at[z], self.x_recv.at[z])
+
+    def to_y(self, z):
+        return self.copy(self.ref(self.at(z)), self.at(self.z, dy=1), self.y_send.at[z], self.y_recv.at[z])
+
+    def on_y(self, z):
+        return self.copy(self.ref(self.at(z, dx=1), 0), self.at(self.z, dy=1), self.dy_send.at[z], self.dy_recv.at[z])
+
+    def on_x(self, z):
+        return self.copy(self.ref(self.at(z, dy=1), 1), self.at(self.z, dx=1), self.dx_send.at[z], self.dx_recv.at[z])
+
+    def spread(self, z, step):
+        if step:
+            self.arrived(self.ref(self.at(z)), self.z_recv.at[z])
+        if step >= 0:
+            @pl.when(self.z > 0)
+            def _():
+                self.down(z).start()
+        if step <= 0:
+            @pl.when(self.z < 3)
+            def _():
+                self.up(z).start()
+        self.to_x(z).start()
+        self.to_y(z).start()
+        self.aside(self.at(z)).start()
+
+    def turn(self, z):
+        self.arrived(self.ref(self.at(z, dx=1)), self.x_recv.at[z])
+        self.on_y(z).start()
+        self.aside(self.at(z, dx=1)).start()
+        self.arrived(self.ref(self.at(z, dy=1)), self.y_recv.at[z])
+        self.on_x(z).start()
+        self.aside(self.at(z, dy=1)).start()
+
+    def corner(self, z):
+        self.arrived(self.ref(self.at(z, 1, 1), 0), self.dy_recv.at[z])
+        self.aside(self.at(z, 1, 1), 0).start()
+        self.arrived(self.ref(self.at(z, 1, 1), 1), self.dx_recv.at[z])
+        self.aside(self.at(z, 1, 1), 1).start()
+
+    def each(self, step, do):
+        z = self.z + step
+
+        @pl.when((z >= 0) & (z < 4))
+        def _():
+            do(z)
 
     def run(self):
         mine = pltpu.make_async_copy(self.w_ref, self.all_ref.at[self.dev], self.l_sem)
         mine.start()
         mine.wait()
-        for i in range(CUTS):
-            self.forward(i).start()
-            self.backward(i).start()
-        for c in range(CUTS):
-            self.aside(self.block, c).start()
-
-        @pl.loop(0, self.f_count)
-        def _(j):
-            shard, c = self.arrived(j, False)
-
-            @pl.when(j + CUTS < self.f_count)
+        for far in range(4):
+            steps = (far, -far) if far else (0,)
+            for step in steps:
+                self.each(step, functools.partial(self.spread, step=step))
+            for step in steps:
+                self.each(step, self.turn)
+        for far in range(4):
+            for step in (far, -far) if far else (0,):
+                self.each(step, self.corner)
+
+        @pl.loop(0, 4)
+        def _(z):
+            @pl.when((z >= self.z) & (self.z > 0))
             def _():
-                self.forward(j + CUTS).start()
-
-            self.aside(shard, c).start()
-
-            @pl.when(j < self.b_count)
+                self.down(z).wait_send()
+
+            @pl.when((z <= self.z) & (self.z < 3))
             def _():
-                shard, c = self.arrived(j, True)
-
-                @pl.when(j + CUTS < self.b_count)
-                def _():
-                    self.backward(j + CUTS).start()
-
-                self.aside(shard, c).start()
-
-        @pl.loop(0, self.f_count)
-        def _(i):
-            self.forward(i).wait_send()
-
-        @pl.loop(0, self.b_count)
-        def _(i):
-            self.backward(i).wait_send()
-
-        @pl.loop(0, self.blocks * CUTS)
-        def _(a):
-            block, c = a // CUTS, lax.rem(a, CUTS)
-            self.aside(block, c).wait_send()
-            ref = self.chunk(block, 1 - self.member, c)
-            pltpu.make_async_remote_copy(
-                src_ref=ref, dst_ref=ref, send_sem=self.s_send.at[a], recv_sem=self.s_recv.at[a],
-                device_id=(self.block, 1 - self.member), device_id_type=MESH,
-            ).wait_recv()
-
-
-def fetch_kernel(blocks, members, ring, *refs):
-    if ring:
+                self.up(z).wait_send()
+
+            for move in (self.to_x, self.to_y, self.on_x, self.on_y):
+                move(z).wait_send()
+            for dy, dx, half in ((0, 0, None), (0, 1, None), (1, 0, None), (1, 1, 0), (1, 1, 1)):
+                self.aside(self.at(z, dy, dx), half).wait_send()
+                self.aside(self.at(z, dy, dx), half, True).wait_recv()
+
+
+def fetch_kernel(blocks, members, grid, *refs):
+    if grid:
         w_ref, refs = refs[0], refs[1:]
         k_ref, v_ref, own_ref, all_ref = refs[:4]
         refs = refs[4:]
@@ -175,8 +181,8 @@
     next_k, next_v = to_next(0, k_ref, pk_ref), to_next(1, v_ref, pv_ref)
     next_k.start()
     next_v.start()
-    if ring:
-        Ring(blocks, w_ref, all_ref, refs[8:]).run()
+    if grid:
+        Grid(w_ref, all_ref, refs[8:]).run()
 
     @pl.when(last)
     def _():
@@ -202,7 +208,7 @@
 def fetch(w, keys, values, own, blocks, members):
     ndev = blocks * members
     dma = pltpu.SemaphoreType.DMA
-    ring = members == 2 and blocks > 2 and w.shape[0] % (16 * CUTS) == 0
+    grid = members == 2 and blocks == 16 and w.shape[0] % 32 == 0
     outs = (
         jax.ShapeDtypeStruct(keys.shape, keys.dtype),
         jax.ShapeDtypeStruct(values.shape, values.dtype),
@@ -210,13 +216,12 @@
     )
     args = (keys, values, own)
     sems = [dma((ndev,)), dma((blocks,)), dma((2,)), dma((2,)), dma]
-    if ring:
+    if grid:
         outs = (jax.ShapeDtypeStruct((ndev,) + w.shape, w.dtype),) + outs
         args = (w,) + args
-        steps = blocks * CUTS
-        sems += [dma((steps,))] * 6 + [dma]
+        sems += [dma((8,))] + [dma((4,))] * 9 + [dma((2 * blocks,))] * 2 + [dma]
     got = pl.pallas_call(
-        functools.partial(fetch_kernel, blocks, members, ring),
+        functools.partial(fetch_kernel, blocks, members, grid),
         out_shape=outs,
         in_specs=[ANY] * len(args),
         out_specs=(ANY,) * len(outs),
@@ -224,7 +229,7 @@
         compiler_params=pltpu.CompilerParams(has_side_effects=True),
         name="fetch",
     )(*args)
-    if ring:
+    if grid:
         return (got[0].reshape(ndev * w.shape[0], w.shape[1]),) + tuple(got[1:])
     return (lax.all_gather(w, ("seq", "fsdp"), axis=0, tiled=True),) + tuple(got)
 

time: 145 us -> 141 us (0.972)
  Pallas kernels: 130 us -> 126 us
    pallas_call x1, Pallas kernels: 78 us -> 71.4 us  [fetch(): pl.pallas_call(functools.partial(fetch_kernel, blocks, members, grid), ou...]
    pallas_call x1, Pallas kernels: 32.7 us -> 35.4 us  [give_back(): pl.pallas_call(functools.partial(give_back_kernel, blocks, members), out_...]
where the time goes in v3:
time: 141 us
  Pallas kernels  126 us (89%)
  local copies, waits for them, and re-layouts  8.5 us (6%)
  other arithmetic  6.01 us (4%)
    pallas_call x1, Pallas kernels, fetch(): pl.pallas_call(functools.partial(fetch_kernel, blocks, members, grid), ou...  71.4 us
    pallas_call x1, Pallas kernels, give_back(): pl.pallas_call(functools.partial(give_back_kernel, blocks, members), out_...  35.4 us
    pallas_call x1, Pallas kernels, attend(): pl.pallas_call(attend_kernel, grid=(width // step,), in_specs=[col, col,...  19 us

profile of v3, /device:TPU:15, one launch (start us, length us, event | category | flops | bytes accessed | tf_op | source)
XLA Modules:
  0.0 141.1 jit_solution(13297249160076368249)
XLA Ops:
  0.6 0.0 copy-start
  0.7 1.2 dynamic_slice.8
  1.9 0.0 copy-done
  1.9 0.2 dynamic-slice_reduce_fusion
  2.1 0.1 compare_reduce_fusion
  2.2 0.7 fusion.11
  3.0 0.8 slice_bitcast_fusion.4
  3.8 0.6 reshape.64.refs_3_
  4.5 0.7 add_convert_fusion.valid_ref
  5.2 71.4 %fetch.1 = (bf16[32,64,2048]{2,1,0:T(8,128)(2,1)}, bf16[128,2048]{1,0:T(8,128)(2,1)}, bf16[128,2048]{1,0:T(8,128)(2,1)}, bf16[16,16,1024]{2,1,0:T(8,128)(2,1)}) custom-call(bf16[64,2048]{1,0:T(8,128)(2,1)} %refs_0_.1, bf16[128,2048]{1,0:T(8,128)(2,1)} %k_ref.1, bf16[128,2048]{1,0:T(8,128)(2,1)} %v_ref.1, bf16[16,1024]{1,0:T(8,128)(2,1)} %reshape.64.refs_3_), custom_call_target="tpu_custom_call" | custom-call | tf_op jit(solution)/shard_map/fetch/pallas_call | solution.py:223
  76.6 1.4 %reshape.65 = bf16[16,2,4,2048]{3,2,1,0:T(4,128)(2,1)S(1)} reshape(bf16[16,16,1024]{2,1,0:T(8,128)(2,1)} %get-tuple-element.18) | data formatting | bytes 1048576 | tf_op jit(solution)/shard_map/reshape | solution.py:403
  78.0 0.2 slice_bitcast_fusion.2
  78.2 0.8 reshape_squeeze.7.vs_ref
  79.0 0.8 reshape_squeeze.6.ks_ref
  79.8 19.0 %attend.1 = (bf16[128,2048]{1,0:T(8,128)(2,1)}, bf16[128,2048]{1,0:T(8,128)(2,1)}, f32[128,2048]{1,0:T(8,128)}, f32[128,2048]{1,0:T(8,128)}, bf16[2,128,2048]{2,...) custom-call(bf16[128,2048]{1,0:T(8,128)(2,1)} %q_ref.1, bf16[128,2048]{1,0:T(8,128)(2,1)} %k_ref.1, bf16[128,2048]{1,0:T(8,128)(2,1)} %v_ref.1, ...), custom_call_target="tpu_custom_call" | custom-call | tf_op jit(solution)/shard_map/attend/pallas_call | solution.py:366
  98.8 1.2 reshape.67
  100.1 0.2 copy.20
  100.3 0.9 reshape.68.gsum_ref
  101.2 35.4 %give_back.1 = (bf16[2,128,2048]{2,1,0:T(8,128)(2,1)}, bf16[32,16,1024]{2,1,0:T(8,128)(2,1)}) custom-call(bf16[2,128,2048]{2,1,0:T(8,128)(2,1)} %get-tuple-element.23.ret_ref, bf16[16,16,1024]{2,1,0:T(8,128)(2,1)} %reshape.68.gsum_ref), custom_call_target="tpu_custom_call" | custom-call | tf_op jit(solution)/shard_map/give_back/pallas_call | solution.py:285
  136.6 0.0 copy-start.1
  136.6 0.0 copy-start.2
  136.6 1.6 %select_reduce_fusion = f32[16,1024]{1,0:T(8,128)S(1)} fusion(bf16[32,16,1024]{2,1,0:T(8,128)(2,1)} %get-tuple-element.26, pred[32]{0:T(512)(128)(4,1)S(1)} %compare_and_fusion), kind=kLoop, calls=%fused_computation.2 | loop fusion | flops 1556480 | bytes 1114144 | tf_op jit(solution)/shard_map/reduce_sum | solution.py:424
  138.3 1.5 %convert_select_fusion = f32[2,128,2048]{2,1,0:T(8,128)S(1)} fusion(bf16[2,128,2048]{2,1,0:T(8,128)(2,1)} %get-tuple-element.25, pred[]{:T(512)S(6)} %lt.30), kind=kLoop, calls=%fused_computation.3 | loop fusion | flops 1048576 | bytes 3145729 | tf_op jit(solution)/shard_map/jit(_where)/select_n | solution.py:422
  139.8 0.0 copy-done.1
  139.8 0.0 copy-done.2
  139.8 1.3 fusion.5
  (8 shorter events, 0.1 us)
Async XLA Ops:
  0.6 1.3 copy-start
  136.6 3.2 %copy-start.1 = (f32[128,2048]{1,0:T(8,128)S(1)}, f32[128,2048]{1,0:T(8,128)}, u32[]{:S(2)}) copy-start(f32[128,2048]{1,0:T(8,128)} %get-tuple-element.22) | copy-start | bytes 3145732
  136.6 3.2 %copy-start.2 = (f32[128,2048]{1,0:T(8,128)S(1)}, f32[128,2048]{1,0:T(8,128)}, u32[]{:S(2)}) copy-start(f32[128,2048]{1,0:T(8,128)} %get-tuple-element.27) | copy-start | bytes 3145732

commit v4 on v3

--- a/solution.py
+++ b/solution.py
@@ -109,7 +109,7 @@
         def _():
             do(z)
 
-    def run(self):
+    def run(self, begin):
         mine = pltpu.make_async_copy(self.w_ref, self.all_ref.at[self.dev], self.l_sem)
         mine.start()
         mine.wait()
@@ -117,6 +117,8 @@
             steps = (far, -far) if far else (0,)
             for step in steps:
                 self.each(step, functools.partial(self.spread, step=step))
+            if far == 0:
+                begin()
             for step in steps:
                 self.each(step, self.turn)
         for far in range(4):
@@ -170,19 +172,24 @@
 
     local = pltpu.make_async_copy(own_ref, sum_ref.at[block], loc_sem)
 
-    @pl.when(last)
-    def _():
-        local.start()
-
-        @pl.loop(0, ndev - 1)
-        def _(i):
-            summary_to(i).start()
-
     next_k, next_v = to_next(0, k_ref, pk_ref), to_next(1, v_ref, pv_ref)
-    next_k.start()
-    next_v.start()
+
+    def begin():
+        @pl.when(last)
+        def _():
+            local.start()
+
+            @pl.loop(0, ndev - 1)
+            def _(i):
+                summary_to(i).start()
+
+        next_k.start()
+        next_v.start()
+
     if grid:
-        Grid(w_ref, all_ref, refs[8:]).run()
+        Grid(w_ref, all_ref, refs[8:]).run(begin)
+    else:
+        begin()
 
     @pl.when(last)
     def _():
@@ -252,13 +259,13 @@
             recv_sem=recv_sem.at[dev], device_id=(m, members - 1), device_id_type=MESH,
         )
 
-    back.start()
-
     @pl.loop(0, blocks)
     def _(m):
         @pl.when(m < block)
         def _():
             part_to(m).start()
+
+    back.start()
 
     @pl.loop(0, blocks)
     def _(m):

time: 141 us -> 144 us (1.021)
  Pallas kernels: 126 us -> 128 us
    pallas_call x1, Pallas kernels: 71.4 us -> 74.2 us  [fetch(): pl.pallas_call(functools.partial(fetch_kernel, blocks, members, grid), ou...]
where the time goes in v4:
time: 144 us
  Pallas kernels  128 us (89%)
  local copies, waits for them, and re-layouts  8.5 us (6%)
  other arithmetic  6.01 us (4%)
    pallas_call x1, Pallas kernels, fetch(): pl.pallas_call(functools.partial(fetch_kernel, blocks, members, grid), ou...  74.2 us
    pallas_call x1, Pallas kernels, give_back(): pl.pallas_call(functools.partial(give_back_kernel, blocks, members), out_...  35.1 us
    pallas_call x1, Pallas kernels, attend(): pl.pallas_call(attend_kernel, grid=(width // step,), in_specs=[col, col,...  19 us

profile of v4, /device:TPU:15, one launch (start us, length us, event | category | flops | bytes accessed | tf_op | source)
XLA Modules:
  0.0 143.6 jit_solution(10103561429534797815)
XLA Ops:
  0.6 0.0 copy-start
  0.7 1.2 dynamic_slice.8
  1.9 0.0 copy-done
  1.9 0.2 dynamic-slice_reduce_fusion
  2.1 0.1 compare_reduce_fusion
  2.2 0.7 fusion.11
  3.0 0.8 slice_bitcast_fusion.4
  3.8 0.6 reshape.64.refs_3_
  4.5 0.7 add_convert_fusion.valid_ref
  5.2 74.2 %fetch.1 = (bf16[32,64,2048]{2,1,0:T(8,128)(2,1)}, bf16[128,2048]{1,0:T(8,128)(2,1)}, bf16[128,2048]{1,0:T(8,128)(2,1)}, bf16[16,16,1024]{2,1,0:T(8,128)(2,1)}) custom-call(bf16[64,2048]{1,0:T(8,128)(2,1)} %refs_0_.1, bf16[128,2048]{1,0:T(8,128)(2,1)} %k_ref.1, bf16[128,2048]{1,0:T(8,128)(2,1)} %v_ref.1, bf16[16,1024]{1,0:T(8,128)(2,1)} %reshape.64.refs_3_), custom_call_target="tpu_custom_call" | custom-call | tf_op jit(solution)/shard_map/fetch/pallas_call | solution.py:230
  79.3 1.4 reshape.65
  80.8 0.2 slice_bitcast_fusion.2
  81.0 0.8 reshape_squeeze.7.vs_ref
  81.8 0.8 reshape_squeeze.6.ks_ref
  82.5 19.0 %attend.1 = (bf16[128,2048]{1,0:T(8,128)(2,1)}, bf16[128,2048]{1,0:T(8,128)(2,1)}, f32[128,2048]{1,0:T(8,128)}, f32[128,2048]{1,0:T(8,128)}, bf16[2,128,2048]{2,...) custom-call(bf16[128,2048]{1,0:T(8,128)(2,1)} %q_ref.1, bf16[128,2048]{1,0:T(8,128)(2,1)} %k_ref.1, bf16[128,2048]{1,0:T(8,128)(2,1)} %v_ref.1, ...), custom_call_target="tpu_custom_call" | custom-call | tf_op jit(solution)/shard_map/attend/pallas_call | solution.py:373
  101.6 1.2 reshape.67
  102.8 0.2 copy.20
  103.1 0.9 reshape.68.gsum_ref
  104.0 35.1 %give_back.1 = (bf16[2,128,2048]{2,1,0:T(8,128)(2,1)}, bf16[32,16,1024]{2,1,0:T(8,128)(2,1)}) custom-call(bf16[2,128,2048]{2,1,0:T(8,128)(2,1)} %get-tuple-element.23.ret_ref, bf16[16,16,1024]{2,1,0:T(8,128)(2,1)} %reshape.68.gsum_ref), custom_call_target="tpu_custom_call" | custom-call | tf_op jit(solution)/shard_map/give_back/pallas_call | solution.py:292
  139.1 0.0 copy-start.1
  139.1 0.0 copy-start.2
  139.1 1.6 %select_reduce_fusion = f32[16,1024]{1,0:T(8,128)S(1)} fusion(bf16[32,16,1024]{2,1,0:T(8,128)(2,1)} %get-tuple-element.26, pred[32]{0:T(512)(128)(4,1)S(1)} %compare_and_fusion), kind=kLoop, calls=%fused_computation.2 | loop fusion | flops 1556480 | bytes 1114144 | tf_op jit(solution)/shard_map/reduce_sum | solution.py:431
  140.8 1.5 %convert_select_fusion = f32[2,128,2048]{2,1,0:T(8,128)S(1)} fusion(bf16[2,128,2048]{2,1,0:T(8,128)(2,1)} %get-tuple-element.25, pred[]{:T(512)S(6)} %lt.30), kind=kLoop, calls=%fused_computation.3 | loop fusion | flops 1048576 | bytes 3145729 | tf_op jit(solution)/shard_map/jit(_where)/select_n | solution.py:429
  142.3 0.0 copy-done.1
  142.3 0.0 copy-done.2
  142.3 1.3 fusion.5
  (8 shorter events, 0.1 us)
Async XLA Ops:
  0.6 1.3 copy-start
  139.1 3.2 %copy-start.1 = (f32[128,2048]{1,0:T(8,128)S(1)}, f32[128,2048]{1,0:T(8,128)}, u32[]{:S(2)}) copy-start(f32[128,2048]{1,0:T(8,128)} %get-tuple-element.22) | copy-start | bytes 3145732
  139.1 3.2 %copy-start.2 = (f32[128,2048]{1,0:T(8,128)S(1)}, f32[128,2048]{1,0:T(8,128)}, u32[]{:S(2)}) copy-start(f32[128,2048]{1,0:T(8,128)} %get-tuple-element.27) | copy-start | bytes 3145732
